TPU v7x, 256 devices: a whole 4x4x8 slice. The times are simulated.
256 devices in a mesh: row: 32 (over z, x_lo, core), col: 8 (over x_hi, y).
Axes of the slice: x: 4 (x_hi: 2, x_lo: 2; x = x_hi * 2 + x_lo), y: 4, z: 8, core: 2. Of those that a mesh axis runs over, the one named last changes fastest.
Arguments:
- queries: bfloat16 [1, 128, 128, 1536], P(None, 'row', 'col'), may hold values from -180 to 180
- key_tokens: bfloat16 [1, 128, 128, 1536], P(None, 'row', 'col'), may hold values from -4 to 4
- values: bfloat16 [1, 128, 128, 1536], P(None, 'row', 'col'), may hold values from -6 to 6
- position_bias: float32 [24, 49], replicated, may hold values from -4 to 4
- out_weight: bfloat16 [1536, 1536], P('col', 'row'), may hold values from -0.15625 to 0.15625
Outputs:
- projected: bfloat16 [1, 128, 128, 1536], P(None, 'row', 'col')
All inputs are finite; a program needn't handle non-finite values.
Results may differ from a plain program's by a relative error of at most 0.0057.
Values may be sent and summed in bfloat16 or wider, within the bound.
No kernel may reach another device: no remote copies, remote signals or barrier semaphores. Data moves between devices by JAX's collectives and lax.ppermute only.
A program may use at most 64 MiB of HBM per device.

v0:
```python
import math
import jax
import jax.numpy as jnp
from jax import lax
from jax.sharding import PartitionSpec as P


def extended_2(block, sides, width):
    for axis, dim in sides:
        count = lax.axis_size(axis)
        forward = [(i, i + 1) for i in range(count - 1)]
        backward = [(target, source) for source, target in forward]
        low = lax.ppermute(
            lax.slice_in_dim(block, block.shape[dim] - width, None, axis=dim), axis, forward
        )
        high = lax.ppermute(lax.slice_in_dim(block, 0, width, axis=dim), axis, backward)
        block = jnp.concatenate([low, block, high], axis=dim)
    return block


def shards(queries, key_tokens, values, position_bias, out_weight):
    images = queries.shape[0]
    band_rows = queries.shape[1]
    strip_cols = queries.shape[2]
    model_width = queries.shape[3]
    head_count = position_bias.shape[0]
    head_size = model_width // head_count
    height = band_rows * lax.axis_size("row")
    breadth = strip_cols * lax.axis_size("col")
    stacked = jnp.stack([key_tokens, values], 0)
    extended = extended_2(stacked, (("row", 2), ("col", 3)), 3)
    key_ext = extended[0]
    value_ext = extended[1]
    query_heads = queries.reshape(images, band_rows, strip_cols, head_count, head_size)
    global_rows = lax.axis_index("row") * band_rows + jnp.arange(band_rows)
    global_cols = lax.axis_index("col") * strip_cols + jnp.arange(strip_cols)
    offsets = jnp.arange(7) - 3
    rows_inside = (global_rows[None, :] + offsets[:, None] >= 0) & (
        global_rows[None, :] + offsets[:, None] < height
    )
    cols_inside = (global_cols[None, :] + offsets[:, None] >= 0) & (
        global_cols[None, :] + offsets[:, None] < breadth
    )
    inside = (rows_inside[:, None, :, None] & cols_inside[None, :, None, :]).reshape(
        49, 1, band_rows, strip_cols, 1
    )
    score_scale = 1.0 / math.sqrt(head_size)
    row_steps = jnp.arange(7, dtype=jnp.int32)

    def score_step(carry, row_off):
        band_keys = lax.dynamic_slice_in_dim(key_ext, row_off, band_rows, 1)
        row_scores = []
        for col_off in range(7):
            window = band_keys[:, :, col_off : col_off + strip_cols].reshape(
                images, band_rows, strip_cols, head_count, head_size
            )
            row_scores.append(
                jnp.einsum(
                    "ibshd,ibshd->ibsh", query_heads, window, preferred_element_type=jnp.float32
                )
            )
        return (carry, jnp.stack(row_scores, 0))

    unused, score_grid = lax.scan(score_step, jnp.zeros((), jnp.float32), row_steps)
    scores = score_grid.reshape(49, images, band_rows, strip_cols, head_count) * score_scale
    scores = scores + jnp.transpose(position_bias)[:, None, None, None, :]
    scores = jnp.where(inside, scores, -jnp.inf)
    attention = jax.nn.softmax(scores, axis=0).astype(jnp.bfloat16)
    attention_grid = attention.reshape(7, 7, images, band_rows, strip_cols, head_count)

    def value_step(summed, items):
        row_off, weights = items
        band_values = lax.dynamic_slice_in_dim(value_ext, row_off, band_rows, 1)
        row_total = None
        for col_off in range(7):
            window = band_values[:, :, col_off : col_off + strip_cols].reshape(
                images, band_rows, strip_cols, head_count, head_size
            )
            term = weights[col_off].astype(jnp.float32)[..., None] * window.astype(jnp.float32)
            row_total = term if row_total is None else row_total + term
        return (summed + row_total, None)

    initial_sum = jnp.zeros((images, band_rows, strip_cols, head_count, head_size), jnp.float32)
    summed, unused_out = lax.scan(value_step, initial_sum, (row_steps, attention_grid))
    mixed_heads = summed.astype(jnp.bfloat16).reshape(images * band_rows * strip_cols, model_width)
    tall_weight = lax.all_gather(out_weight, "col", axis=0, tiled=True)
    result = jnp.dot(
        mixed_heads,
        lax.all_gather(tall_weight, "row", axis=1, tiled=True),
        preferred_element_type=jnp.float32,
    )
    return result.astype(jnp.bfloat16).reshape(images, band_rows, strip_cols, model_width)


def solution(mesh):
    in_specs = (
        P(None, "row", "col", None),
        P(None, "row", "col", None),
        P(None, "row", "col", None),
        P(),
        P("col", "row"),
    )
    out_specs = P(None, "row", "col", None)
    return jax.shard_map(shards, mesh=mesh, in_specs=in_specs, out_specs=out_specs, check_vma=False)
```

profile of v0, /device:TPU:248, one launch (start us, length us, event | category | flops | bytes accessed | tf_op | source)
XLA Modules:
  0.0 312.8 jit_solution(8154622619189542940)
XLA Ops:
  9.8 4.5 %collective-permute-start.1 = (bf16[2,1,3,16,1536]{4,3,2,1,0:T(8,128)(2,1)S(1)}, bf16[2,1,3,16,1536]{4,3,2,1,0:T(8,128)(2,1)S(1)}, u32[]{:S(2)}, u32[]{:S(2)}) collective-permute-start(bf16[2,1,3,16,1536]{4,3,2,1,0:T(8,128)(2,1)S(1)} %get-tuple-element.132), channel_id=1, source_target_pairs={{8,0},{16,8},{24,16},{32,24},{40,32},{48,40},{56,48},{64,56},{72,6... | collective-permute-start | bytes 884744 | tf_op jit(solution)/shard_map/ppermute | solution.py:16
  14.3 34.5 %all-gather = bf16[8,192,48]{1,2,0:T(8,128)(2,1)S(1)} all-gather(bf16[1,192,48]{1,2,0:T(8,128)(2,1)} %bitcast.136), channel_id=1, replica_groups=mesh['row'=32,'col'=8] {'col'}, dimensions={0}, use_global_device_ids=true | all-gather | bytes 165888 | tf_op jit(solution)/shard_map/all_gather | solution.py:86
  51.3 4.6 %collective-permute-start.2 = (bf16[2,1,10,3,1536]{4,3,2,1,0:T(4,128)(2,1)S(1)}, bf16[2,1,10,3,1536]{4,3,2,1,0:T(4,128)(2,1)S(1)}, u32[]{:S(2)}, u32[]{:S(2)}) collective-permute-start(bf16[2,1,10,3,1536]{4,3,2,1,0:T(4,128)(2,1)S(1)} %get-tuple-element.129), channel_id=1, source_target_pairs={{0,1},{1,2},{2,3},{3,4},{4,5},{5,6},{6,7},{8,9},{9,10},{10,11},{11... | collective-permute-start | bytes 552968 | tf_op jit(solution)/shard_map/ppermute | solution.py:13
  59.7 9.8 %collective-permute-done.3 = bf16[2,1,10,3,1536]{4,3,2,1,0:T(4,128)(2,1)S(1)} collective-permute-done((bf16[2,1,10,3,1536]{4,3,2,1,0:T(4,128)(2,1)S(1)}, bf16[2,1,10,3,1536]{4,3,2,1,0:T(4,128)(2,1)S(1)}, u32[]{:S(2)}, u32[]{:S(2)}) %collective-permute-start.3) | collective-permute-done | bytes 184352 | tf_op jit(solution)/shard_map/ppermute | solution.py:16
  70.3 93.0 %while.21 = (s32[]{:T(128)}, f32[7,7,1,4,16,24]{5,4,3,2,1,0:T(8,128)}, s32[7]{0:T(128)S(1)}, bf16[1,10,22,1536]{3,2,1,0:T(8,128)(2,1)S(1)}, bf16[1,4,16,24,64]{4...) while((s32[]{:T(128)}, ...), condition=%wide.region_1.2_spmd, body=%wide.region_0.1_spmd.sunk | while | flops 2151947 | bytes 7826199 | solution.py:64
  80.0 2.7 fusion.23
  93.3 2.7 fusion.23
  106.6 2.8 fusion.23
  119.9 2.7 fusion.23
  133.2 2.7 fusion.23
  146.5 2.7 fusion.23
  159.8 2.7 fusion.23
  166.8 2.6 divide_convert_fusion
  169.4 130.5 %while.22 = (s32[]{:T(128)}, f32[1,4,16,24,64]{4,3,2,1,0:T(8,128)}, bf16[7,7,1,4,16,24]{5,4,3,2,1,0:T(8,128)(2,1)}, s32[7]{0:T(128)S(1)}, bf16[1,10,22,1536]{3,2...) while((s32[]{:T(128)}, f32[1,4,16,24,64]{4,3,2,1,0:T(8,128)}, ...), condition=%wide.region_5.6_spmd.clone, body=%wide.region_4.5_spmd.clone.sunk | while | flops 2173452 | bytes 13280573 | solution.py:84
  177.1 2.1 reshape.517
  179.2 2.1 reshape.518
  183.3 4.7 %select_add_fusion.2 = f32[1,4,16,24,64]{4,3,2,1,0:T(8,128)} fusion(f32[1,4,16,24,64]{4,3,2,1,0:T(8,128)} %get-tuple-element.308, f32[1,4,16,24,64]{4,3,2,1,0:T(8,128)S(1)} %reshape.513, f32[1,4,16,24,64]{4,3,2,1,0:T(8,128)S(1)} %reshape.514, f32[1,4,16,24,64]{4,3,2,1,0:T(8,128)S(1)} %reshape.515, f32[1,4,16,24,64]{4,3,2,1,0:T(8,128)} %reshape.516, ...), kind=kLoop, calls=%fused_computation.clone.1 | loop fusion | flops 1474560 | bytes 3581953 | tf_op jit(solution)/shard_map/while/body/eval_jaxpr/add | solution.py:81
  197.7 2.1 reshape.518
  201.8 4.8 %select_add_fusion.2 = f32[1,4,16,24,64]{4,3,2,1,0:T(8,128)} fusion(f32[1,4,16,24,64]{4,3,2,1,0:T(8,128)} %get-tuple-element.308, f32[1,4,16,24,64]{4,3,2,1,0:T(8,128)S(1)} %reshape.513, f32[1,4,16,24,64]{4,3,2,1,0:T(8,128)S(1)} %reshape.514, f32[1,4,16,24,64]{4,3,2,1,0:T(8,128)S(1)} %reshape.515, f32[1,4,16,24,64]{4,3,2,1,0:T(8,128)} %reshape.516, ...), kind=kLoop, calls=%fused_computation.clone.1 | loop fusion | flops 1474560 | bytes 3581953 | tf_op jit(solution)/shard_map/while/body/eval_jaxpr/add | solution.py:81
  216.4 2.1 reshape.518
  220.5 4.8 %select_add_fusion.2 = f32[1,4,16,24,64]{4,3,2,1,0:T(8,128)} fusion(f32[1,4,16,24,64]{4,3,2,1,0:T(8,128)} %get-tuple-element.308, f32[1,4,16,24,64]{4,3,2,1,0:T(8,128)S(1)} %reshape.513, f32[1,4,16,24,64]{4,3,2,1,0:T(8,128)S(1)} %reshape.514, f32[1,4,16,24,64]{4,3,2,1,0:T(8,128)S(1)} %reshape.515, f32[1,4,16,24,64]{4,3,2,1,0:T(8,128)} %reshape.516, ...), kind=kLoop, calls=%fused_computation.clone.1 | loop fusion | flops 1474560 | bytes 3581953 | tf_op jit(solution)/shard_map/while/body/eval_jaxpr/add | solution.py:81
  235.0 2.1 reshape.518
  239.1 4.8 %select_add_fusion.2 = f32[1,4,16,24,64]{4,3,2,1,0:T(8,128)} fusion(f32[1,4,16,24,64]{4,3,2,1,0:T(8,128)} %get-tuple-element.308, f32[1,4,16,24,64]{4,3,2,1,0:T(8,128)S(1)} %reshape.513, f32[1,4,16,24,64]{4,3,2,1,0:T(8,128)S(1)} %reshape.514, f32[1,4,16,24,64]{4,3,2,1,0:T(8,128)S(1)} %reshape.515, f32[1,4,16,24,64]{4,3,2,1,0:T(8,128)} %reshape.516, ...), kind=kLoop, calls=%fused_computation.clone.1 | loop fusion | flops 1474560 | bytes 3581953 | tf_op jit(solution)/shard_map/while/body/eval_jaxpr/add | solution.py:81
  251.5 2.1 reshape.517
  253.7 2.1 reshape.518
  257.8 4.8 %select_add_fusion.2 = f32[1,4,16,24,64]{4,3,2,1,0:T(8,128)} fusion(f32[1,4,16,24,64]{4,3,2,1,0:T(8,128)} %get-tuple-element.308, f32[1,4,16,24,64]{4,3,2,1,0:T(8,128)S(1)} %reshape.513, f32[1,4,16,24,64]{4,3,2,1,0:T(8,128)S(1)} %reshape.514, f32[1,4,16,24,64]{4,3,2,1,0:T(8,128)S(1)} %reshape.515, f32[1,4,16,24,64]{4,3,2,1,0:T(8,128)} %reshape.516, ...), kind=kLoop, calls=%fused_computation.clone.1 | loop fusion | flops 1474560 | bytes 3581953 | tf_op jit(solution)/shard_map/while/body/eval_jaxpr/add | solution.py:81
  270.2 2.1 reshape.517
  272.3 2.1 reshape.518
  276.4 4.8 %select_add_fusion.2 = f32[1,4,16,24,64]{4,3,2,1,0:T(8,128)} fusion(f32[1,4,16,24,64]{4,3,2,1,0:T(8,128)} %get-tuple-element.308, f32[1,4,16,24,64]{4,3,2,1,0:T(8,128)S(1)} %reshape.513, f32[1,4,16,24,64]{4,3,2,1,0:T(8,128)S(1)} %reshape.514, f32[1,4,16,24,64]{4,3,2,1,0:T(8,128)S(1)} %reshape.515, f32[1,4,16,24,64]{4,3,2,1,0:T(8,128)} %reshape.516, ...), kind=kLoop, calls=%fused_computation.clone.1 | loop fusion | flops 1474560 | bytes 3581953 | tf_op jit(solution)/shard_map/while/body/eval_jaxpr/add | solution.py:81
  291.0 2.1 reshape.518
  295.1 4.8 %select_add_fusion.2 = f32[1,4,16,24,64]{4,3,2,1,0:T(8,128)} fusion(f32[1,4,16,24,64]{4,3,2,1,0:T(8,128)} %get-tuple-element.308, f32[1,4,16,24,64]{4,3,2,1,0:T(8,128)S(1)} %reshape.513, f32[1,4,16,24,64]{4,3,2,1,0:T(8,128)S(1)} %reshape.514, f32[1,4,16,24,64]{4,3,2,1,0:T(8,128)S(1)} %reshape.515, f32[1,4,16,24,64]{4,3,2,1,0:T(8,128)} %reshape.516, ...), kind=kLoop, calls=%fused_computation.clone.1 | loop fusion | flops 1474560 | bytes 3581953 | tf_op jit(solution)/shard_map/while/body/eval_jaxpr/add | solution.py:81
  301.4 4.5 %convolution_convert_fusion = bf16[64,1536]{1,0:T(8,128)(2,1)} fusion(bf16[64,1536]{1,0:T(8,128)(2,1)S(1)} %reshape.439, bf16[1536,1536]{0,1:T(8,128)(2,1)} %all-gather.3.cloned.1.call-done), kind=kOutput, calls=%fused_computation.51 | convolution fusion | flops 302088192 | bytes 5111808 | tf_op jit(solution)/shard_map/dot_general | solution.py:87
  (218 shorter events, 136.6 us)
Async XLA Ops:
  6.5 44.6 %copy-start = (bf16[1,4,16,1536]{3,2,1,0:T(8,128)(2,1)S(1)}, bf16[1,4,16,1536]{3,2,1,0:T(8,128)(2,1)}, u32[]{:S(2)}) copy-start(bf16[1,4,16,1536]{3,2,1,0:T(8,128)(2,1)} %param.10) | copy-start | bytes 589828
  6.5 44.6 %copy-start.1 = (bf16[1,4,16,1536]{3,2,1,0:T(8,128)(2,1)S(1)}, bf16[1,4,16,1536]{3,2,1,0:T(8,128)(2,1)}, u32[]{:S(2)}) copy-start(bf16[1,4,16,1536]{3,2,1,0:T(8,128)(2,1)} %param.11) | copy-start | bytes 589828
  6.5 43.3 %copy-start.2 = (bf16[1,4,16,1536]{3,2,1,0:T(8,128)(2,1)S(1)}, bf16[1,4,16,1536]{3,2,1,0:T(8,128)(2,1)}, u32[]{:S(2)}) copy-start(bf16[1,4,16,1536]{3,2,1,0:T(8,128)(2,1)} %param.9) | copy-start | bytes 589828
  6.5 44.3 %copy-start.3 = (f32[24,49]{1,0:T(8,128)S(1)}, f32[24,49]{1,0:T(8,128)}, u32[]{:S(2)}) copy-start(f32[24,49]{1,0:T(8,128)} %param.12) | copy-start | bytes 14116
  6.5 294.8 %all-gather.3.cloned.1.call-start = ((), (), s32[]{:S(2)}) async-start(), calls=%async_computation | async-start | bytes 4866048 | tf_op jit(solution)/shard_map/all_gather | solution.py:89
  7.8 43.2 %collective-permute-start = (bf16[2,1,3,16,1536]{4,3,2,1,0:T(8,128)(2,1)S(1)}, bf16[2,1,3,16,1536]{4,3,2,1,0:T(8,128)(2,1)S(1)}, u32[]{:S(2)}, u32[]{:S(2)}) collective-permute-start(bf16[2,1,3,16,1536]{4,3,2,1,0:T(8,128)(2,1)S(1)} %get-tuple-element.131), channel_id=1, source_target_pairs={{0,8},{8,16},{16,24},{24,32},{32,40},{40,48},{48,56},{56,64},{64,7... | collective-permute-start | bytes 884744 | tf_op jit(solution)/shard_map/ppermute | solution.py:13
  9.8 41.3 %collective-permute-start.1 = (bf16[2,1,3,16,1536]{4,3,2,1,0:T(8,128)(2,1)S(1)}, bf16[2,1,3,16,1536]{4,3,2,1,0:T(8,128)(2,1)S(1)}, u32[]{:S(2)}, u32[]{:S(2)}) collective-permute-start(bf16[2,1,3,16,1536]{4,3,2,1,0:T(8,128)(2,1)S(1)} %get-tuple-element.132), channel_id=1, source_target_pairs={{8,0},{16,8},{24,16},{32,24},{40,32},{48,40},{56,48},{64,56},{72,6... | collective-permute-start | bytes 884744 | tf_op jit(solution)/shard_map/ppermute | solution.py:16
  51.3 8.3 %collective-permute-start.2 = (bf16[2,1,10,3,1536]{4,3,2,1,0:T(4,128)(2,1)S(1)}, bf16[2,1,10,3,1536]{4,3,2,1,0:T(4,128)(2,1)S(1)}, u32[]{:S(2)}, u32[]{:S(2)}) collective-permute-start(bf16[2,1,10,3,1536]{4,3,2,1,0:T(4,128)(2,1)S(1)} %get-tuple-element.129), channel_id=1, source_target_pairs={{0,1},{1,2},{2,3},{3,4},{4,5},{5,6},{6,7},{8,9},{9,10},{10,11},{11... | collective-permute-start | bytes 552968 | tf_op jit(solution)/shard_map/ppermute | solution.py:13
  56.0 13.5 %collective-permute-start.3 = (bf16[2,1,10,3,1536]{4,3,2,1,0:T(4,128)(2,1)S(1)}, bf16[2,1,10,3,1536]{4,3,2,1,0:T(4,128)(2,1)S(1)}, u32[]{:S(2)}, u32[]{:S(2)}) collective-permute-start(bf16[2,1,10,3,1536]{4,3,2,1,0:T(4,128)(2,1)S(1)} %get-tuple-element.130), channel_id=1, source_target_pairs={{1,0},{2,1},{3,2},{4,3},{5,4},{6,5},{7,6},{9,8},{10,9},{11,10},{12... | collective-permute-start | bytes 552968 | tf_op jit(solution)/shard_map/ppermute | solution.py:16
Sparse Core Ops, SparseCore 0:
  49.9 67.5 all-gather.2
where the time goes:
time: 316 us; the launch traced here: 313 us
  local copies, waits for them, and re-layouts  129 us (41%)
  other arithmetic  78.6 us (25%)
  blocking collectives  34.5 us (11%)
  loops' own time  28.2 us (9%)
  between operations  13.6 us (4%)
  starting transfers between devices  13.1 us (4%)
  waiting for transfers between devices  11.5 us (4%)
  matrix products  4.55 us (1%)
    convert_element_type x49, local copies, waits for them, and re-layouts, value_step(): window.astype(jnp.float32)  62.9 us
    another operation x49, local copies, waits for them, and re-layouts  42.4 us
    all_gather x1, blocking collectives, shards(): tall_weight = lax.all_gather(out_weight, 'col', axis=0, tiled=True)  34.5 us
    add x7, other arithmetic, value_step(): return (summed + row_total, None)  33.4 us
    dot_general x7, other arithmetic, score_step(): jnp.einsum('ibshd,ibshd->ibsh', query_heads, window, preferred_element_ty...  19.2 us
    another operation x1, loops' own time, shards(): lax.scan(score_step, jnp.zeros((), jnp.float32), row_steps)  14.3 us
    another operation x1, loops' own time, shards(): lax.scan(value_step, initial_sum, (row_steps, attention_grid))  13.9 us
    convert_element_type x7, other arithmetic, value_step(): window.astype(jnp.float32)  10.4 us
  transfers between devices with their start and end apart: 5, of which 2 were waited for; matrix products, arithmetic and copies ran while one was open for 66% of the time, Pallas kernels for 0%

commit v1 on v0

--- a/solution.py
+++ b/solution.py
@@ -3,6 +3,12 @@
 import jax.numpy as jnp
 from jax import lax
 from jax.sharding import PartitionSpec as P
+
+
+def convert_signs(patch, join_dim):
+    work_now = lax.all_to_all(jnp.stack([patch] * lax.axis_size("row")), "row", 0, 0)
+    o_now = jnp.concatenate(work_now, axis=join_dim)
+    return o_now
 
 
 def extended_2(block, sides, width):
@@ -84,11 +90,7 @@
     summed, unused_out = lax.scan(value_step, initial_sum, (row_steps, attention_grid))
     mixed_heads = summed.astype(jnp.bfloat16).reshape(images * band_rows * strip_cols, model_width)
     tall_weight = lax.all_gather(out_weight, "col", axis=0, tiled=True)
-    result = jnp.dot(
-        mixed_heads,
-        lax.all_gather(tall_weight, "row", axis=1, tiled=True),
-        preferred_element_type=jnp.float32,
-    )
+    result = jnp.dot(mixed_heads, convert_signs(tall_weight, 1), preferred_element_type=jnp.float32)
     return result.astype(jnp.bfloat16).reshape(images, band_rows, strip_cols, model_width)
 
 

time: 316 us -> 336 us (1.063)
  the two profiles are of different devices: /device:TPU:248 before, /device:TPU:25 now
where the time goes in v1:
time: 336 us; the launch traced here: 332 us
  local copies, waits for them, and re-layouts  135 us (40%)
  other arithmetic  81.2 us (24%)
  blocking collectives  30.8 us (9%)
  loops' own time  28.1 us (8%)
  starting transfers between devices  27.9 us (8%)
  waiting for transfers between devices  24.5 us (7%)
  matrix products  4.55 us (1%)
    convert_element_type x49, local copies, waits for them, and re-layouts, value_step(): window.astype(jnp.float32)  61.9 us
    another operation x49, local copies, waits for them, and re-layouts  42.4 us
    add x7, other arithmetic, value_step(): return (summed + row_total, None)  33.8 us
    all_gather x1, blocking collectives, shards(): tall_weight = lax.all_gather(out_weight, 'col', axis=0, tiled=True)  30.8 us
    dot_general x7, other arithmetic, score_step(): jnp.einsum('ibshd,ibshd->ibsh', query_heads, window, preferred_element_ty...  19.1 us
    all_to_all x1, starting transfers between devices, convert_signs(): lax.all_to_all(jnp.stack([patch] * lax.axis_size('row')), 'row', 0, 0)  15.3 us
    another operation x1, loops' own time, shards(): lax.scan(score_step, jnp.zeros((), jnp.float32), row_steps)  14.3 us
    ppermute x2, waiting for transfers between devices, extended_2(): lax.ppermute(lax.slice_in_dim(block, block.shape[dim] - width, None, axis...  14.2 us
  transfers between devices with their start and end apart: 5, of which 2 were waited for; matrix products, arithmetic and copies ran while one was open for 65% of the time, Pallas kernels for 0%

profile of v1, /device:TPU:25, one launch (start us, length us, event | category | flops | bytes accessed | tf_op | source)
XLA Modules:
  0.0 331.9 jit_solution(17330656322159591841)
XLA Ops:
  1.2 3.7 %collective-permute-start = (bf16[2,1,3,16,1536]{4,3,2,1,0:T(8,128)(2,1)S(1)}, bf16[2,1,3,16,1536]{4,3,2,1,0:T(8,128)(2,1)S(1)}, u32[]{:S(2)}, u32[]{:S(2)}) collective-permute-start(bf16[2,1,3,16,1536]{4,3,2,1,0:T(8,128)(2,1)S(1)} %get-tuple-element.131), channel_id=1, source_target_pairs={{0,8},{8,16},{16,24},{24,32},{32,40},{40,48},{48,56},{56,64},{64,7... | collective-permute-start | bytes 884744 | tf_op jit(solution)/shard_map/ppermute | solution.py:19
  6.8 30.8 %all-gather = bf16[8,192,48]{1,2,0:T(8,128)(2,1)S(1)} all-gather(bf16[1,192,48]{1,2,0:T(8,128)(2,1)} %bitcast.139), channel_id=1, replica_groups=mesh['row'=32,'col'=8] {'col'}, dimensions={0}, use_global_device_ids=true | all-gather | bytes 165888 | tf_op jit(solution)/shard_map/all_gather | solution.py:92
  37.9 2.7 stack.35
  40.6 15.3 %all-to-all-start = ((bf16[32,1536,48]{1,2,0:T(8,128)(2,1)}), bf16[32,1536,48]{1,2,0:T(8,128)(2,1)}, u32[]{:S(2)}, u32[]{:S(2)}) async-start(bf16[32,1536,48]{1,2,0:T(8,128)(2,1)} %stack.35), calls=%async_computation | async-start | bytes 9437184 | tf_op jit(solution)/shard_map/all_to_all | solution.py:9
  57.4 5.1 %collective-permute-start.2 = (bf16[2,1,10,3,1536]{4,3,2,1,0:T(4,128)(2,1)S(1)}, bf16[2,1,10,3,1536]{4,3,2,1,0:T(4,128)(2,1)S(1)}, u32[]{:S(2)}, u32[]{:S(2)}) collective-permute-start(bf16[2,1,10,3,1536]{4,3,2,1,0:T(4,128)(2,1)S(1)} %get-tuple-element.129), channel_id=1, source_target_pairs={{0,1},{1,2},{2,3},{3,4},{4,5},{5,6},{6,7},{8,9},{9,10},{10,11},{11... | collective-permute-start | bytes 552968 | tf_op jit(solution)/shard_map/ppermute | solution.py:19
  64.6 14.2 %collective-permute-done.2 = bf16[2,1,10,3,1536]{4,3,2,1,0:T(4,128)(2,1)S(1)} collective-permute-done((bf16[2,1,10,3,1536]{4,3,2,1,0:T(4,128)(2,1)S(1)}, bf16[2,1,10,3,1536]{4,3,2,1,0:T(4,128)(2,1)S(1)}, u32[]{:S(2)}, u32[]{:S(2)}) %collective-permute-start.2) | collective-permute-done | bytes 184352 | tf_op jit(solution)/shard_map/ppermute | solution.py:19
  78.8 10.3 %collective-permute-done.3 = bf16[2,1,10,3,1536]{4,3,2,1,0:T(4,128)(2,1)S(1)} collective-permute-done((bf16[2,1,10,3,1536]{4,3,2,1,0:T(4,128)(2,1)S(1)}, bf16[2,1,10,3,1536]{4,3,2,1,0:T(4,128)(2,1)S(1)}, u32[]{:S(2)}, u32[]{:S(2)}) %collective-permute-start.3) | collective-permute-done | bytes 184352 | tf_op jit(solution)/shard_map/ppermute | solution.py:22
  89.9 92.9 %while.21 = (s32[]{:T(128)}, f32[7,7,1,4,16,24]{5,4,3,2,1,0:T(8,128)}, s32[7]{0:T(128)S(1)}, bf16[1,10,22,1536]{3,2,1,0:T(8,128)(2,1)S(1)}, bf16[1,4,16,24,64]{4...) while((s32[]{:T(128)}, ...), condition=%wide.region_1.2_spmd, body=%wide.region_0.1_spmd.sunk | while | flops 2151947 | bytes 7825699 | solution.py:70
  99.6 2.7 fusion.23
  112.9 2.7 fusion.23
  126.2 2.7 fusion.23
  139.4 2.7 fusion.23
  152.7 2.7 fusion.23
  166.0 2.7 fusion.23
  179.2 2.7 fusion.23
  187.4 138.6 %while.22 = (s32[]{:T(128)}, f32[1,4,16,24,64]{4,3,2,1,0:T(8,128)}, bf16[7,7,1,4,16,24]{5,4,3,2,1,0:T(8,128)(2,1)}, s32[7]{0:T(128)}, bf16[1,10,22,1536]{3,2,1,0...) while((s32[]{:T(128)}, f32[1,4,16,24,64]{4,3,2,1,0:T(8,128)}, ...), condition=%wide.region_5.6_spmd.clone, body=%wide.region_4.5_spmd.clone.sunk | while | flops 2173452 | bytes 13280581 | solution.py:90
  199.1 2.1 reshape.528
  202.3 4.7 %select_add_fusion.2 = f32[1,4,16,24,64]{4,3,2,1,0:T(8,128)} fusion(f32[1,4,16,24,64]{4,3,2,1,0:T(8,128)} %get-tuple-element.308, f32[1,4,16,24,64]{4,3,2,1,0:T(8,128)S(1)} %reshape.523, f32[1,4,16,24,64]{4,3,2,1,0:T(8,128)S(1)} %reshape.524, f32[1,4,16,24,64]{4,3,2,1,0:T(8,128)S(1)} %reshape.525, f32[1,4,16,24,64]{4,3,2,1,0:T(8,128)} %reshape.526, ...), kind=kLoop, calls=%fused_computation.clone.1 | loop fusion | flops 1474560 | bytes 3581953 | tf_op jit(solution)/shard_map/while/body/eval_jaxpr/add | solution.py:87
  218.8 2.1 reshape.528
  222.0 4.8 %select_add_fusion.2 = f32[1,4,16,24,64]{4,3,2,1,0:T(8,128)} fusion(f32[1,4,16,24,64]{4,3,2,1,0:T(8,128)} %get-tuple-element.308, f32[1,4,16,24,64]{4,3,2,1,0:T(8,128)S(1)} %reshape.523, f32[1,4,16,24,64]{4,3,2,1,0:T(8,128)S(1)} %reshape.524, f32[1,4,16,24,64]{4,3,2,1,0:T(8,128)S(1)} %reshape.525, f32[1,4,16,24,64]{4,3,2,1,0:T(8,128)} %reshape.526, ...), kind=kLoop, calls=%fused_computation.clone.1 | loop fusion | flops 1474560 | bytes 3581953 | tf_op jit(solution)/shard_map/while/body/eval_jaxpr/add | solution.py:87
  238.6 2.1 reshape.528
  241.8 4.8 %select_add_fusion.2 = f32[1,4,16,24,64]{4,3,2,1,0:T(8,128)} fusion(f32[1,4,16,24,64]{4,3,2,1,0:T(8,128)} %get-tuple-element.308, f32[1,4,16,24,64]{4,3,2,1,0:T(8,128)S(1)} %reshape.523, f32[1,4,16,24,64]{4,3,2,1,0:T(8,128)S(1)} %reshape.524, f32[1,4,16,24,64]{4,3,2,1,0:T(8,128)S(1)} %reshape.525, f32[1,4,16,24,64]{4,3,2,1,0:T(8,128)} %reshape.526, ...), kind=kLoop, calls=%fused_computation.clone.1 | loop fusion | flops 1474560 | bytes 3581953 | tf_op jit(solution)/shard_map/while/body/eval_jaxpr/add | solution.py:87
  258.5 2.1 reshape.528
  261.6 4.8 %select_add_fusion.2 = f32[1,4,16,24,64]{4,3,2,1,0:T(8,128)} fusion(f32[1,4,16,24,64]{4,3,2,1,0:T(8,128)} %get-tuple-element.308, f32[1,4,16,24,64]{4,3,2,1,0:T(8,128)S(1)} %reshape.523, f32[1,4,16,24,64]{4,3,2,1,0:T(8,128)S(1)} %reshape.524, f32[1,4,16,24,64]{4,3,2,1,0:T(8,128)S(1)} %reshape.525, f32[1,4,16,24,64]{4,3,2,1,0:T(8,128)} %reshape.526, ...), kind=kLoop, calls=%fused_computation.clone.1 | loop fusion | flops 1474560 | bytes 3581953 | tf_op jit(solution)/shard_map/while/body/eval_jaxpr/add | solution.py:87
  274.1 2.1 reshape.526
  278.3 2.1 reshape.528
  281.4 4.8 %select_add_fusion.2 = f32[1,4,16,24,64]{4,3,2,1,0:T(8,128)} fusion(f32[1,4,16,24,64]{4,3,2,1,0:T(8,128)} %get-tuple-element.308, f32[1,4,16,24,64]{4,3,2,1,0:T(8,128)S(1)} %reshape.523, f32[1,4,16,24,64]{4,3,2,1,0:T(8,128)S(1)} %reshape.524, f32[1,4,16,24,64]{4,3,2,1,0:T(8,128)S(1)} %reshape.525, f32[1,4,16,24,64]{4,3,2,1,0:T(8,128)} %reshape.526, ...), kind=kLoop, calls=%fused_computation.clone.1 | loop fusion | flops 1474560 | bytes 3581953 | tf_op jit(solution)/shard_map/while/body/eval_jaxpr/add | solution.py:87
  298.1 2.1 reshape.528
  301.2 4.8 %select_add_fusion.2 = f32[1,4,16,24,64]{4,3,2,1,0:T(8,128)} fusion(f32[1,4,16,24,64]{4,3,2,1,0:T(8,128)} %get-tuple-element.308, f32[1,4,16,24,64]{4,3,2,1,0:T(8,128)S(1)} %reshape.523, f32[1,4,16,24,64]{4,3,2,1,0:T(8,128)S(1)} %reshape.524, f32[1,4,16,24,64]{4,3,2,1,0:T(8,128)S(1)} %reshape.525, f32[1,4,16,24,64]{4,3,2,1,0:T(8,128)} %reshape.526, ...), kind=kLoop, calls=%fused_computation.clone.1 | loop fusion | flops 1474560 | bytes 3581953 | tf_op jit(solution)/shard_map/while/body/eval_jaxpr/add | solution.py:87
  317.9 2.1 reshape.528
  321.1 4.8 %select_add_fusion.2 = f32[1,4,16,24,64]{4,3,2,1,0:T(8,128)} fusion(f32[1,4,16,24,64]{4,3,2,1,0:T(8,128)} %get-tuple-element.308, f32[1,4,16,24,64]{4,3,2,1,0:T(8,128)S(1)} %reshape.523, f32[1,4,16,24,64]{4,3,2,1,0:T(8,128)S(1)} %reshape.524, f32[1,4,16,24,64]{4,3,2,1,0:T(8,128)S(1)} %reshape.525, f32[1,4,16,24,64]{4,3,2,1,0:T(8,128)} %reshape.526, ...), kind=kLoop, calls=%fused_computation.clone.1 | loop fusion | flops 1474560 | bytes 3581953 | tf_op jit(solution)/shard_map/while/body/eval_jaxpr/add | solution.py:87
  327.4 4.5 %convolution_convert_fusion = bf16[64,1536]{1,0:T(8,128)(2,1)} fusion(bf16[64,1536]{1,0:T(8,128)(2,1)S(1)} %reshape.447, bf16[1536,1536]{0,1:T(8,128)(2,1)} %bitcast.17), kind=kOutput, calls=%fused_computation.51 | convolution fusion | flops 302088192 | bytes 5111808 | tf_op jit(solution)/shard_map/dot_general | solution.py:93
  (220 shorter events, 147.3 us)
Async XLA Ops:
  1.2 56.0 %collective-permute-start = (bf16[2,1,3,16,1536]{4,3,2,1,0:T(8,128)(2,1)S(1)}, bf16[2,1,3,16,1536]{4,3,2,1,0:T(8,128)(2,1)S(1)}, u32[]{:S(2)}, u32[]{:S(2)}) collective-permute-start(bf16[2,1,3,16,1536]{4,3,2,1,0:T(8,128)(2,1)S(1)} %get-tuple-element.131), channel_id=1, source_target_pairs={{0,8},{8,16},{16,24},{24,32},{32,40},{40,48},{48,56},{56,64},{64,7... | collective-permute-start | bytes 884744 | tf_op jit(solution)/shard_map/ppermute | solution.py:19
  4.9 52.3 %collective-permute-start.1 = (bf16[2,1,3,16,1536]{4,3,2,1,0:T(8,128)(2,1)S(1)}, bf16[2,1,3,16,1536]{4,3,2,1,0:T(8,128)(2,1)S(1)}, u32[]{:S(2)}, u32[]{:S(2)}) collective-permute-start(bf16[2,1,3,16,1536]{4,3,2,1,0:T(8,128)(2,1)S(1)} %get-tuple-element.132), channel_id=1, source_target_pairs={{8,0},{16,8},{24,16},{32,24},{40,32},{48,40},{56,48},{64,56},{72,6... | collective-permute-start | bytes 884744 | tf_op jit(solution)/shard_map/ppermute | solution.py:22
  40.6 15.3 %copy-start.4 = (f32[24,49]{1,0:T(8,128)S(1)}, f32[24,49]{1,0:T(8,128)}, u32[]{:S(2)}) copy-start(f32[24,49]{1,0:T(8,128)} %param.12) | copy-start | bytes 14116
  40.6 15.4 %copy-start.3 = (bf16[1,4,16,1536]{3,2,1,0:T(8,128)(2,1)S(1)}, bf16[1,4,16,1536]{3,2,1,0:T(8,128)(2,1)}, u32[]{:S(2)}) copy-start(bf16[1,4,16,1536]{3,2,1,0:T(8,128)(2,1)} %param.9) | copy-start | bytes 589828
  40.6 16.6 %copy-start.1 = (bf16[1,4,16,1536]{3,2,1,0:T(8,128)(2,1)S(1)}, bf16[1,4,16,1536]{3,2,1,0:T(8,128)(2,1)}, u32[]{:S(2)}) copy-start(bf16[1,4,16,1536]{3,2,1,0:T(8,128)(2,1)} %param.10) | copy-start | bytes 589828
  40.6 16.6 %copy-start.2 = (bf16[1,4,16,1536]{3,2,1,0:T(8,128)(2,1)S(1)}, bf16[1,4,16,1536]{3,2,1,0:T(8,128)(2,1)}, u32[]{:S(2)}) copy-start(bf16[1,4,16,1536]{3,2,1,0:T(8,128)(2,1)} %param.11) | copy-start | bytes 589828
  40.6 286.8 %all-to-all-start = ((bf16[32,1536,48]{1,2,0:T(8,128)(2,1)}), bf16[32,1536,48]{1,2,0:T(8,128)(2,1)}, u32[]{:S(2)}, u32[]{:S(2)}) async-start(bf16[32,1536,48]{1,2,0:T(8,128)(2,1)} %stack.35), calls=%async_computation | async-start | bytes 9437184 | tf_op jit(solution)/shard_map/all_to_all | solution.py:9
  57.4 21.4 %collective-permute-start.2 = (bf16[2,1,10,3,1536]{4,3,2,1,0:T(4,128)(2,1)S(1)}, bf16[2,1,10,3,1536]{4,3,2,1,0:T(4,128)(2,1)S(1)}, u32[]{:S(2)}, u32[]{:S(2)}) collective-permute-start(bf16[2,1,10,3,1536]{4,3,2,1,0:T(4,128)(2,1)S(1)} %get-tuple-element.129), channel_id=1, source_target_pairs={{0,1},{1,2},{2,3},{3,4},{4,5},{5,6},{6,7},{8,9},{9,10},{10,11},{11... | collective-permute-start | bytes 552968 | tf_op jit(solution)/shard_map/ppermute | solution.py:19
  62.5 26.5 %collective-permute-start.3 = (bf16[2,1,10,3,1536]{4,3,2,1,0:T(4,128)(2,1)S(1)}, bf16[2,1,10,3,1536]{4,3,2,1,0:T(4,128)(2,1)S(1)}, u32[]{:S(2)}, u32[]{:S(2)}) collective-permute-start(bf16[2,1,10,3,1536]{4,3,2,1,0:T(4,128)(2,1)S(1)} %get-tuple-element.130), channel_id=1, source_target_pairs={{1,0},{2,1},{3,2},{4,3},{5,4},{6,5},{7,6},{9,8},{10,9},{11,10},{12... | collective-permute-start | bytes 552968 | tf_op jit(solution)/shard_map/ppermute | solution.py:22
  182.8 1.9 copy-start
